TPU v7x, 32 devices: a whole 2x2x4 slice. The times are simulated.
32 devices in a mesh: seq: 4 (over x, core), head: 8 (over z, y).
Axes of the slice: x: 2, y: 2, z: 4, core: 2. Of those that a mesh axis runs over, the one named last changes fastest.
Arguments:
- queries: bfloat16 [512, 8192], P('seq', 'head'), may hold values from -256 to 256
- key_rows: bfloat16 [512, 128], P('seq'), may hold values from -6 to 6
- value_rows: bfloat16 [512, 128], P('seq'), may hold values from -6 to 6
- pair_keys: bfloat16 [512, 128], P('seq'), may hold values from 0.27 to 1.73
- pair_values: bfloat16 [512, 128], P('seq'), may hold values from 0.099609375 to 1.8984375
- first_key: int32 [512], P('seq'), may hold values from 0 to 511, as said below
- residual: float32 [512, 8192], P(('seq', 'head')), may hold values from -6 to 6
- out_weight: bfloat16 [8192, 8192], P('head', 'seq'), may hold values from -0.25 to 0.25
Outputs:
- updated: float32 [512, 8192], P(('seq', 'head'))
Inputs may be any that keep to these rules, and one draw needn't show every extreme that they name: first_key never falls along the tokens, first_key[i] <= i, and first_key[i] = i where a document begins; positions 0 and 511 begin one.
All inputs are finite; a program needn't handle non-finite values.
Results may differ from a plain program's by a relative error of at most 0.005.
Values may be sent and summed in bfloat16 or wider, within the bound.
No kernel may reach another device: no remote copies, remote signals or barrier semaphores. Data moves between devices by JAX's collectives and lax.ppermute only.
A program may use at most 128 MiB of HBM per device.

v0:
```python
import functools
import math

import jax
import jax.numpy as jnp
from jax import lax
from jax.experimental import pallas as pl
from jax.experimental.pallas import tpu as pltpu
from jax.sharding import PartitionSpec as P

DH = 128
W1 = 512
W2 = 32
BLOCK = 128
LOW = -1e30
TILE = 8
GROUP = 4
GROUPS = 4
RUN = 2
ROWS = TILE * W2


def attention_kernel(
    token_at, skip, steps, most, tok, own_ref, base_ref, first_ref, q_hbm, ctx_hbm, *rest,
    held,
):
    if held:
        w_hbm, out_ref, w_out, *rest = rest
    else:
        out_ref, *rest = rest
    q_ref, ctx_ref, qf, of, pkf, pk2, pvb, kx, vx, lhs, scores, weights, arrived = rest
    copies = [
        pltpu.make_async_copy(source, target, arrived.at[index])
        for index, (source, target) in enumerate(
            [(ctx_hbm, ctx_ref), (q_hbm, q_ref)]
        )
    ]
    if held:
        weight = pltpu.make_async_copy(w_hbm, w_out, arrived.at[2])
        weight.start()
    for copy in copies:
        copy.start()
    unit = GROUP * ROWS
    row = lax.broadcasted_iota(jnp.int32, (unit, DH), 0)
    col = lax.broadcasted_iota(jnp.int32, (unit, DH), 1)
    pick = jnp.where(row // TILE == col, 1.0, 0.0).astype(jnp.bfloat16)
    for g in range(GROUPS):
        lhs[g * unit : (g + 1) * unit, DH:] = pick
    for copy in copies:
        copy.wait()
    blocks = kx.shape[1] // BLOCK
    own = own_ref[0]
    base = base_ref[0]
    origin = base - own * tok
    for b in range(blocks):
        rows = slice(b * BLOCK, (b + 1) * BLOCK)
        for g in range(GROUPS):
            kx[g, rows, :DH] = ctx_ref[rows, :DH]
        vx[rows, :DH] = ctx_ref[rows, DH : 2 * DH]
        vx[rows, DH:] = jnp.ones((BLOCK, DH), jnp.bfloat16)
    before = pl.multiple_of(jnp.maximum(own * tok - W2, 0), W2)
    pkf[0:W2] = ctx_ref[pl.ds(before, W2), 2 * DH :].astype(jnp.float32)
    pkf[W2 : W2 + tok] = ctx_ref[pl.ds(pl.multiple_of(own * tok, BLOCK), tok), 2 * DH :].astype(jnp.float32)
    pkf[W2 + tok :] = jnp.zeros((8, 2 * DH), jnp.float32)

    def spread(blk, _):
        r0 = pl.multiple_of(blk * 8, 8)
        x = pkf[pl.ds(r0, 16)]
        for r in range(8):
            a = jnp.broadcast_to(x[r : r + 1, :DH], (TILE, DH))
            b = jnp.broadcast_to(x[r + 1 : r + 2, :DH], (TILE, DH))
            pk2[r0 + r] = jnp.concatenate([a, b], axis=0).astype(jnp.bfloat16)
            pvb[r0 + r] = jnp.broadcast_to(x[r : r + 1, DH:], (TILE, DH))
        return 0

    lax.fori_loop(0, (W2 + tok) // 8, spread, 0)
    for h in range(TILE):
        qf[pl.ds(h, tok, stride=TILE), :] = q_ref[:, h * DH : (h + 1) * DH].astype(jnp.float32)
    lane = lax.broadcasted_iota(jnp.int32, (1, DH), 1)
    lane_token = lane // W2
    lane_offset = lane % W2
    factor = math.log2(math.e) / math.sqrt(DH)
    tokens = GROUP * GROUPS

    def step(index, _):
        begin = [
            token_at + (index * (GROUPS // RUN) + g // RUN) * skip + g % RUN * GROUP
            for g in range(GROUPS)
        ]
        pos0 = base + begin[0]
        first = [first_ref[begin[t // GROUP] + t % GROUP] for t in range(tokens)]
        lowest = jnp.maximum(first[0], pos0 - W1 + 1)
        block_low = (lowest - origin) // BLOCK
        block_high = (base + begin[-1] + GROUP - 1 - origin) // BLOCK
        start = pl.multiple_of(block_low * BLOCK, BLOCK)

        def run(n):
            keys = n * BLOCK
            key_pos = lax.broadcasted_iota(jnp.int32, (keys, DH), 0) + (origin + start)

            def score(g):
                mine = first[g * GROUP : (g + 1) * GROUP]
                first_lane = jnp.full((1, DH), mine[-1], jnp.int32)
                for t in range(GROUP - 2, -1, -1):
                    first_lane = jnp.where(lane_token == t, mine[t], first_lane)
                high = base + begin[g] + lane_token
                low = jnp.maximum(first_lane, high - W1 + 1)
                low = jnp.where(high - (W2 - 1) + lane_offset >= first_lane, low, 2**30)
                ok = (key_pos >= low) & (key_pos <= high)
                kx[g, pl.ds(start, keys), DH:] = jnp.where(ok, 0.0, LOW).astype(jnp.bfloat16)
                for t in range(g * GROUP, (g + 1) * GROUP):
                    token = begin[g] + t % GROUP
                    q = qf[pl.ds(pl.multiple_of(token * TILE, TILE), TILE)]
                    q = jnp.concatenate([q, q], axis=0).astype(jnp.bfloat16)
                    for k in range(W2 // 2):
                        at = t * ROWS + k * 16
                        lhs[at : at + 16, :DH] = q * pk2[token + 1 + 2 * k]
                scores[g * unit : (g + 1) * unit, :keys] = lax.dot_general(
                    lhs[g * unit : (g + 1) * unit],
                    kx[g, pl.ds(start, keys)],
                    (((1,), (1,)), ((), ())),
                    preferred_element_type=jnp.float32,
                )

            def soften(g):
                for t in range(g * GROUP, (g + 1) * GROUP):
                    rows = slice(t * ROWS, (t + 1) * ROWS)
                    s = scores[rows, :keys].reshape(W2, TILE, keys)
                    top = jnp.max(jnp.max(s, axis=0), axis=1, keepdims=True)
                    e = jnp.exp2((s - top[None]) * factor)
                    weights[rows, :keys] = e.reshape(ROWS, keys).astype(jnp.bfloat16)

            def value(g):
                o = jnp.dot(
                    weights[g * unit : (g + 1) * unit, :keys],
                    vx[pl.ds(start, keys)],
                    preferred_element_type=jnp.float32,
                )
                for t in range(GROUP):
                    carried = jnp.zeros((TILE, DH), jnp.float32)
                    total = jnp.zeros((TILE, DH), jnp.float32)
                    for w in range(W2):
                        at = t * ROWS + w * TILE
                        carried += o[at : at + TILE, :DH] * pvb[begin[g] + t + 1 + w]
                        total += o[at : at + TILE, DH:]
                    at = pl.multiple_of((index * tokens + g * GROUP + t) * TILE, TILE)
                    of[pl.ds(at, TILE)] = carried / total

            score(0)
            for g in range(GROUPS):
                if g + 1 < GROUPS:
                    score(g + 1)
                soften(g)
                if g >= 1:
                    value(g - 1)
            value(GROUPS - 1)

        for n in range(1, most + 1):
            pl.when(block_high - block_low + 1 == n)(functools.partial(run, n))
        return 0

    count = steps * GROUP * RUN
    lax.fori_loop(0, count // tokens, step, 0)
    for h in range(TILE):
        out_ref[:, h * DH : (h + 1) * DH] = of[pl.ds(h, count, stride=TILE), :].astype(jnp.bfloat16)
    if held:
        weight.wait()


def attention(token_at, skip, steps, own, base, first_key, q, context, held=None):
    tok = first_key.shape[0]
    count = steps * GROUP * RUN
    rows = context.shape[0]
    span = W1 + (GROUPS // RUN - 1) * skip + RUN * GROUP - 1
    most = min(rows // BLOCK, (span + BLOCK - 2) // BLOCK + 1)
    f32, bf16 = jnp.float32, jnp.bfloat16
    unit = GROUPS * GROUP * ROWS
    more = [] if held is None else [held]
    out = pl.pallas_call(
        functools.partial(attention_kernel, token_at, skip, steps, most, tok, held=held is not None),
        out_shape=[jax.ShapeDtypeStruct((count, TILE * DH), bf16)]
        + [jax.ShapeDtypeStruct(value.shape, value.dtype) for value in more],
        in_specs=[pl.BlockSpec(memory_space=pltpu.SMEM)] * 3
        + [pl.BlockSpec(memory_space=pl.ANY)] * (2 + len(more)),
        out_specs=[pl.BlockSpec(memory_space=pltpu.VMEM)]
        + [pl.BlockSpec(memory_space=pl.ANY) for value in more],
        scratch_shapes=[
            pltpu.VMEM(q.shape, bf16),
            pltpu.VMEM(context.shape, bf16),
            pltpu.VMEM((tok * TILE, DH), f32),
            pltpu.VMEM((count * TILE, DH), f32),
            pltpu.VMEM((W2 + tok + 8, 2 * DH), f32),
            pltpu.VMEM((W2 + tok, 2 * TILE, DH), bf16),
            pltpu.VMEM((W2 + tok, TILE, DH), f32),
            pltpu.VMEM((GROUPS, rows, 2 * DH), bf16),
            pltpu.VMEM((rows, 2 * DH), bf16),
            pltpu.VMEM((unit, 2 * DH), bf16),
            pltpu.VMEM((unit, most * BLOCK), f32),
            pltpu.VMEM((unit, most * BLOCK), bf16),
            pltpu.SemaphoreType.DMA((3,)),
        ],
        cost_estimate=pl.CostEstimate(
            flops=4 * count * ROWS * most * BLOCK * 2 * DH, bytes_accessed=2**20, transcendentals=0
        ),
        compiler_params=pltpu.CompilerParams(vmem_limit_bytes=30 * 2**20),
        name="attention",
    )(own, base, first_key, q, context, *more)
    return out if more else out[0]


def project_kernel(order, split, w_ref, *refs):
    me, head = lax.axis_index("seq"), lax.axis_index("head")
    bits = [head % 2, head // 2 % 2]
    kept_ref, came_ref, *outs, rows_ref = refs
    count = kept_ref.shape[1]
    pieces = [ref.at[i] for ref in (kept_ref, came_ref) for i in range(ref.shape[0])]
    for other, piece in zip(order, pieces, strict=True):
        at = pl.multiple_of((me ^ other) * count, count)
        rows_ref[pl.ds(at, count)] = piece[...]
    columns = w_ref.shape[1]

    def product(start, width):
        return jnp.dot(
            rows_ref[...], w_ref[:, pl.ds(start, width)], preferred_element_type=jnp.float32
        )

    if not split:
        width = math.gcd(columns, 512)
        for at in range(0, columns, width):
            outs[0][:, at : at + width] = jnp.dot(
                rows_ref[...], w_ref[:, at : at + width], preferred_element_type=jnp.float32
            ).astype(jnp.bfloat16)
        return
    sum_ref, *sent_refs = outs
    quarter = columns // 4
    for index, sent_ref in enumerate(sent_refs):
        mine = bits[index]
        start = pl.multiple_of(index * 2 * quarter + (1 - mine) * quarter, 128)
        sent_ref[...] = product(start, quarter).astype(jnp.bfloat16)
    for index in range(len(sent_refs)):
        mine = bits[index]
        start = pl.multiple_of(index * 2 * quarter + mine * quarter, 128)
        sum_ref[:, index * quarter : (index + 1) * quarter] = product(start, quarter)


def swapped(value, axis, bit):
    return lax.ppermute(value, axis, [(a, a ^ bit) for a in range(lax.axis_size(axis))])


def project(features, out_weight, split=False):
    size = lax.axis_size("seq")
    kept, order, bit = features[None], [0], size // 2
    while bit:
        came = swapped(kept, "seq", bit)
        order = order + [other ^ bit for other in order]
        bit //= 2
        if bit:
            kept = jnp.concatenate([kept, came], axis=0)
    rows = size * features.shape[0]
    depth, columns = out_weight.shape
    shapes = jax.ShapeDtypeStruct((rows, columns), jnp.bfloat16)
    memory = pl.BlockSpec(memory_space=pltpu.VMEM)
    if split:
        shapes = [jax.ShapeDtypeStruct((rows, columns // 2), jnp.float32)]
        shapes += [jax.ShapeDtypeStruct((rows, columns // 4), jnp.bfloat16)] * 2
    return pl.pallas_call(
        functools.partial(project_kernel, order, split),
        out_shape=shapes,
        in_specs=[pl.BlockSpec(memory_space=pltpu.VMEM)] * 3,
        out_specs=[memory] * 3 if split else memory,
        scratch_shapes=[pltpu.VMEM((rows, depth), jnp.bfloat16)],
        cost_estimate=pl.CostEstimate(
            flops=2 * rows * depth * columns, bytes_accessed=2 * depth * columns, transcendentals=0
        ),
        compiler_params=pltpu.CompilerParams(vmem_limit_bytes=20 * 2**20),
        name="project",
    )(out_weight, kept, came)


def context_blocks(block, reach):
    count = lax.axis_size("seq")
    if count <= reach + 1:
        return lax.all_gather(block, "seq", axis=0, tiled=True), lax.axis_index("seq")
    pieces = [
        lax.ppermute(block, "seq", [(a, a + steps) for a in range(count - steps)])
        for steps in range(reach, 0, -1)
    ]
    return jnp.concatenate(pieces + [block], axis=0), jnp.int32(reach)


def local(queries, key_rows, value_rows, pair_keys, pair_values, first_key, residual, out_weight):
    tok = queries.shape[0]
    width = queries.shape[1]
    seq_size, head_size = lax.axis_size("seq"), lax.axis_size("head")
    block = jnp.concatenate([key_rows, value_rows, pair_keys, pair_values], axis=1)
    context, own = context_blocks(block, (W1 + tok - 1) // tok)
    base = lax.axis_index("seq") * tok
    own, base = (jnp.asarray(value, jnp.int32).reshape(1) for value in (own, base))
    tile = TILE * DH

    step = GROUP * RUN

    def attend(start, skip, steps, base):
        parts = []
        for at in range(0, width, tile):
            q = queries[:, at : at + tile]
            if q.shape[1] < tile:
                q = jnp.pad(q, ((0, 0), (0, tile - q.shape[1])))
            parts.append(attention(start, skip, steps, own, base, first_key, q, context))
        return (parts[0] if len(parts) == 1 else jnp.concatenate(parts, axis=1))[:, :width]

    columns = out_weight.shape[1]
    rows = tok // head_size

    def product(features, count, split=False):
        rows_out = project(features, out_weight, split)
        return rows_out if split else rows_out.reshape(seq_size * head_size, count, columns)

    def add_pairs(kept, came):
        rows_out = (kept + jnp.concatenate(came, axis=1).astype(jnp.float32)).astype(jnp.bfloat16)
        return rows_out.reshape(seq_size * head_size, -1, columns // 2)

    def exchange(sent):
        return lax.all_to_all(sent, ("seq", "head"), 0, 0)

    def total(got):
        got = got.reshape(seq_size, head_size, -1, columns).astype(jnp.float32)
        return jnp.swapaxes(jnp.sum(got, axis=1), 0, 1).reshape(-1, seq_size * columns)

    def total_split(got):
        quarter = columns // 4
        got = got.reshape(seq_size, head_size // 4, 2, 2, -1, 2, quarter).astype(jnp.float32)
        near = jnp.sum(got[..., 0, :], axis=(1, 2))
        far = jnp.sum(got[..., 1, :], axis=(1, 3))
        both = jnp.stack([near, far], axis=1)
        return jnp.moveaxis(both, 3, 0).reshape(-1, seq_size * columns)

    if rows != 2 * step or head_size % 4:
        sent = product(attend(0, step, tok // step, base), rows)
        return residual + total(exchange(sent))
    steps = tok // rows
    first = attend(0, rows, steps, base)
    sent = product(first, step)
    base, sent = lax.optimization_barrier((base, sent))
    got_first = exchange(sent)
    second = attend(step, rows, steps, base)
    kept, *leaving = product(second, step, True)
    came = [swapped(value, "head", bit) for value, bit in zip(leaving, (1, 2), strict=True)]
    sent, got_first = lax.optimization_barrier((add_pairs(kept, came), got_first))
    got_second = exchange(sent)
    return residual + jnp.concatenate([total(got_first), total_split(got_second)], axis=0)


def solution(mesh):
    placed = (
        P("seq", "head"),
        P("seq", None),
        P("seq", None),
        P("seq", None),
        P("seq", None),
        P("seq"),
        P(("seq", "head"), None),
        P("head", "seq"),
    )
    return jax.shard_map(
        local, mesh=mesh, in_specs=placed, out_specs=P(("seq", "head"), None), check_vma=False
    )
```

profile of v0, /device:TPU:0, one launch (start us, length us, event | category | flops | bytes accessed | tf_op | source)
XLA Modules:
  0.0 91.5 jit_solution(6157571170942942828)
XLA Ops:
  0.0 0.8 pad_maximum_fusion.3
  0.8 8.6 %all_gather.3.ctx_hbm = bf16[512,512]{1,0:T(8,128)(2,1)S(1)} all-gather(bf16[128,512]{1,0:T(8,128)(2,1)S(1)} %pad_maximum_fusion.3), channel_id=1, replica_groups=mesh['seq'=4,'head'=8] {'seq'}, dimensions={0}, use_global_device_ids=true | all-gather | bytes 655360 | tf_op jit(solution)/shard_map/all_gather | solution.py:283
  9.4 0.0 copy-start.2
  9.4 0.9 %copy-done.2 = bf16[128,1024]{1,0:T(8,128)(2,1)S(1)} copy-done((bf16[128,1024]{1,0:T(8,128)(2,1)S(1)}, bf16[128,1024]{1,0:T(8,128)(2,1)}, u32[]{:S(2)}) %copy-start.2) | copy-done | bytes 262168
  10.4 0.0 copy-start.4
  10.4 0.7 copy-done.4
  11.1 0.0 copy-start
  11.1 7.0 %attention.2 = bf16[64,1024]{1,0:T(8,128)(2,1)S(1)} custom-call(s32[1]{0:T(128)} %bitcast.own_ref, s32[1]{0:T(128)} %bitcast.1.base_ref, s32[128]{0:T(128)S(1)} %copy-done.4, bf16[128,1024]{1,0:T(8,128)(2,1)S(1)} %copy-done.2, bf16[512,512]{1,0:T(8,128)(2,1)S(1)} %all_gather.3.ctx_hbm), custom_call_target="tpu_custom_call" | custom-call | flops 8589934592 | bytes 1048576 | tf_op jit(solution)/shard_map/attention/pallas_call | solution.py:179
  18.1 0.0 copy-start.3
  18.1 0.0 copy-start.5
  18.1 6.5 %collective-permute-start = (bf16[1,64,1024]{2,1,0:T(8,128)(2,1)S(1)}, bf16[1,64,1024]{2,1,0:T(8,128)(2,1)S(1)}, u32[]{:S(2)}, u32[]{:S(2)}) collective-permute-start(bf16[1,64,1024]{2,1,0:T(8,128)(2,1)S(1)} %bitcast.22), channel_id=1, source_target_pairs={{0,16},{8,24},{16,0},{24,8},{1,17},{9,25},{17,1},{25,9},{2,18},{10... | collective-permute-start | bytes 393224 | tf_op jit(solution)/shard_map/ppermute | solution.py:247
  24.6 2.9 %collective-permute-done = bf16[1,64,1024]{2,1,0:T(8,128)(2,1)S(1)} collective-permute-done((bf16[1,64,1024]{2,1,0:T(8,128)(2,1)S(1)}, bf16[1,64,1024]{2,1,0:T(8,128)(2,1)S(1)}, u32[]{:S(2)}, u32[]{:S(2)}) %collective-permute-start) | collective-permute-done | bytes 131104 | tf_op jit(solution)/shard_map/ppermute | solution.py:247
  27.6 0.1 collective-permute-start.1
  27.7 1.5 %collective-permute-done.1.refs_1_ = bf16[2,64,1024]{2,1,0:T(8,128)(2,1)S(1)} collective-permute-done((bf16[2,64,1024]{2,1,0:T(8,128)(2,1)S(1)}, bf16[2,64,1024]{2,1,0:T(8,128)(2,1)S(1)}, u32[]{:S(2)}, u32[]{:S(2)}) %collective-permute-start.1) | collective-permute-done | bytes 262176 | tf_op jit(solution)/shard_map/ppermute | solution.py:247
  29.2 0.0 copy-done
  29.2 2.3 %project.2 = bf16[256,2048]{1,0:T(8,128)(2,1)} custom-call(bf16[1024,2048]{1,0:T(8,128)(2,1)S(1)} %copy-done, bf16[2,64,1024]{2,1,0:T(8,128)(2,1)S(1)} %pad_maximum_fusion.refs_0_, bf16[2,64,1024]{2,1,0:T(8,128)(2,1)S(1)} %collective-permute-done.1.refs_1_), custom_call_target="tpu_custom_call" | custom-call | flops 1073741824 | bytes 4194304 | tf_op jit(solution)/shard_map/project/pallas_call | solution.py:266
  31.5 6.6 %all-to-all-start = ((bf16[32,8,2048]{2,1,0:T(8,128)(2,1)}), bf16[32,8,2048]{2,1,0:T(8,128)(2,1)S(1)}, u32[]{:S(2)}, u32[]{:S(2)}) async-start(bf16[32,8,2048]{2,1,0:T(8,128)(2,1)} %bitcast.3), calls=%async_computation | async-start | bytes 2097152 | tf_op jit(solution)/shard_map/all_to_all | solution.py:324
  38.1 0.0 copy-done.3
  38.1 0.0 copy-done.5
  38.1 0.0 copy-start.1
  38.1 7.0 %attention.3 = bf16[64,1024]{1,0:T(8,128)(2,1)S(1)} custom-call(s32[1]{0:T(128)} %bitcast.own_ref, s32[1]{0:T(128)} %bitcast.1.base_ref, s32[128]{0:T(128)S(1)} %copy-done.5, bf16[128,1024]{1,0:T(8,128)(2,1)S(1)} %copy-done.3, bf16[512,512]{1,0:T(8,128)(2,1)S(1)} %all_gather.3.ctx_hbm), custom_call_target="tpu_custom_call" | custom-call | flops 8589934592 | bytes 1048576 | tf_op jit(solution)/shard_map/attention/pallas_call | solution.py:179
  45.1 5.7 %collective-permute-start.2 = (bf16[1,64,1024]{2,1,0:T(8,128)(2,1)S(1)}, bf16[1,64,1024]{2,1,0:T(8,128)(2,1)S(1)}, u32[]{:S(2)}, u32[]{:S(2)}) collective-permute-start(bf16[1,64,1024]{2,1,0:T(8,128)(2,1)S(1)} %bitcast.20), channel_id=1, source_target_pairs={{0,16},{8,24},{16,0},{24,8},{1,17},{9,25},{17,1},{25,9},{2,18},{10... | collective-permute-start | bytes 393224 | tf_op jit(solution)/shard_map/ppermute | solution.py:247
  50.8 3.6 %collective-permute-done.2 = bf16[1,64,1024]{2,1,0:T(8,128)(2,1)S(1)} collective-permute-done((bf16[1,64,1024]{2,1,0:T(8,128)(2,1)S(1)}, bf16[1,64,1024]{2,1,0:T(8,128)(2,1)S(1)}, u32[]{:S(2)}, u32[]{:S(2)}) %collective-permute-start.2) | collective-permute-done | bytes 131104 | tf_op jit(solution)/shard_map/ppermute | solution.py:247
  54.4 0.1 collective-permute-start.3
  54.5 1.5 %collective-permute-done.3.refs_1_ = bf16[2,64,1024]{2,1,0:T(8,128)(2,1)S(1)} collective-permute-done((bf16[2,64,1024]{2,1,0:T(8,128)(2,1)S(1)}, bf16[2,64,1024]{2,1,0:T(8,128)(2,1)S(1)}, u32[]{:S(2)}, u32[]{:S(2)}) %collective-permute-start.3) | collective-permute-done | bytes 262176 | tf_op jit(solution)/shard_map/ppermute | solution.py:247
  56.0 0.0 copy-done.1
  56.0 1.3 %project.3 = (f32[256,1024]{1,0:T(8,128)S(1)}, bf16[256,512]{1,0:T(8,128)(2,1)S(1)}, bf16[256,512]{1,0:T(8,128)(2,1)S(1)}) custom-call(bf16[1024,2048]{1,0:T(8,128)(2,1)S(1)} %copy-done.1, bf16[2,64,1024]{2,1,0:T(8,128)(2,1)S(1)} %pad_maximum_fusion.1.refs_0_, bf16[2,64,1024]{2,1,0:T(8,128)(2,1)S(1)} %collective-permute-done.3.refs_1_), custom_call_target="tpu_custom_call" | custom-call | flops 1073741824 | bytes 4194304 | tf_op jit(solution)/shard_map/project/pallas_call | solution.py:266
  57.3 0.0 copy-start.6
  57.4 1.1 %collective-permute-start.4 = (bf16[256,512]{1,0:T(8,128)(2,1)S(1)}, bf16[256,512]{1,0:T(8,128)(2,1)S(1)}, u32[]{:S(2)}, u32[]{:S(2)}) collective-permute-start(bf16[256,512]{1,0:T(8,128)(2,1)S(1)} %get-tuple-element.14), channel_id=1, source_target_pairs={{0,1},{1,0},{2,3},{3,2},{4,5},{5,4},{6,7},{7,6},{8,9},{9,8},{10,11... | collective-permute-start | bytes 786440 | tf_op jit(solution)/shard_map/ppermute | solution.py:247
  58.4 2.4 %collective-permute-start.5 = (bf16[256,512]{1,0:T(8,128)(2,1)S(1)}, bf16[256,512]{1,0:T(8,128)(2,1)S(1)}, u32[]{:S(2)}, u32[]{:S(2)}) collective-permute-start(bf16[256,512]{1,0:T(8,128)(2,1)S(1)} %get-tuple-element.15), channel_id=1, source_target_pairs={{0,2},{1,3},{2,0},{3,1},{4,6},{5,7},{6,4},{7,5},{8,10},{9,11},{10,... | collective-permute-start | bytes 786440 | tf_op jit(solution)/shard_map/ppermute | solution.py:247
  60.9 5.7 %collective-permute-done.4 = bf16[256,512]{1,0:T(8,128)(2,1)S(1)} collective-permute-done((bf16[256,512]{1,0:T(8,128)(2,1)S(1)}, bf16[256,512]{1,0:T(8,128)(2,1)S(1)}, u32[]{:S(2)}, u32[]{:S(2)}) %collective-permute-start.4) | collective-permute-done | bytes 262176 | tf_op jit(solution)/shard_map/ppermute | solution.py:247
  66.5 2.4 %collective-permute-done.5 = bf16[256,512]{1,0:T(8,128)(2,1)S(1)} collective-permute-done((bf16[256,512]{1,0:T(8,128)(2,1)S(1)}, bf16[256,512]{1,0:T(8,128)(2,1)S(1)}, u32[]{:S(2)}, u32[]{:S(2)}) %collective-permute-start.5) | collective-permute-done | bytes 262176 | tf_op jit(solution)/shard_map/ppermute | solution.py:247
  68.9 0.9 %fusion = bf16[32,8,1024]{2,1,0:T(8,128)(2,1)} fusion(f32[256,1024]{1,0:T(8,128)S(1)} %get-tuple-element.13, bf16[256,512]{1,0:T(8,128)(2,1)S(1)} %collective-permute-done.5, bf16[256,512]{1,0:T(8,128)(2,1)S(1)} %collective-permute-done.4), kind=kLoop, calls=%fused_computation.2 | loop fusion | flops 1572864 | bytes 2097152 | tf_op jit(solution)/shard_map/reshape | solution.py:321
  69.9 0.0 all-to-all-done
  69.9 4.1 %all-to-all-start.1 = ((bf16[32,8,1024]{2,1,0:T(8,128)(2,1)}), bf16[32,8,1024]{2,1,0:T(8,128)(2,1)S(1)}, u32[]{:S(2)}, u32[]{:S(2)}) async-start(bf16[32,8,1024]{2,1,0:T(8,128)(2,1)} %fusion), calls=%async_computation.1 | async-start | bytes 1048576 | tf_op jit(solution)/shard_map/all_to_all | solution.py:324
  74.0 0.2 convert_reduce_fusion
  74.1 16.2 %all-to-all-done.1 = bf16[32,8,1024]{2,1,0:T(8,128)(2,1)S(1)} async-done(((bf16[32,8,1024]{2,1,0:T(8,128)(2,1)}), bf16[32,8,1024]{2,1,0:T(8,128)(2,1)S(1)}, u32[]{:S(2)}, u32[]{:S(2)}) %all-to-all-start.1) | async-done | bytes 524320 | tf_op jit(solution)/shard_map/all_to_all | solution.py:324
  90.3 0.1 convert.2
  90.4 0.1 slice_reduce_fusion.1
  90.6 0.0 copy-done.6
  90.6 0.9 maximum_add_fusion
  (3 shorter events, 0.1 us)
Async XLA Ops:
  9.4 0.9 %copy-start.2 = (bf16[128,1024]{1,0:T(8,128)(2,1)S(1)}, bf16[128,1024]{1,0:T(8,128)(2,1)}, u32[]{:S(2)}) copy-start(bf16[128,1024]{1,0:T(8,128)(2,1)} %q_hbm.3) | copy-start | bytes 786436
  10.4 0.7 copy-start.4
  11.1 18.2 %copy-start = (bf16[1024,2048]{1,0:T(8,128)(2,1)S(1)}, bf16[1024,2048]{1,0:T(8,128)(2,1)}, u32[]{:S(2)}) copy-start(bf16[1024,2048]{1,0:T(8,128)(2,1)} %w_ref.3) | copy-start | bytes 12582916
  18.1 20.0 %copy-start.3 = (bf16[128,1024]{1,0:T(8,128)(2,1)S(1)}, bf16[128,1024]{1,0:T(8,128)(2,1)}, u32[]{:S(2)}) copy-start(bf16[128,1024]{1,0:T(8,128)(2,1)} %q_hbm.3) | copy-start | bytes 786436
  18.1 20.0 %copy-start.5 = (s32[128]{0:T(128)S(1)}, s32[128]{0:T(128)}, u32[]{:S(2)}) copy-start(s32[128]{0:T(128)} %first_ref.3) | copy-start | bytes 1540
  18.1 9.5 %collective-permute-start = (bf16[1,64,1024]{2,1,0:T(8,128)(2,1)S(1)}, bf16[1,64,1024]{2,1,0:T(8,128)(2,1)S(1)}, u32[]{:S(2)}, u32[]{:S(2)}) collective-permute-start(bf16[1,64,1024]{2,1,0:T(8,128)(2,1)S(1)} %bitcast.22), channel_id=1, source_target_pairs={{0,16},{8,24},{16,0},{24,8},{1,17},{9,25},{17,1},{25,9},{2,18},{10... | collective-permute-start | bytes 393224 | tf_op jit(solution)/shard_map/ppermute | solution.py:247
  27.6 1.6 %collective-permute-start.1 = (bf16[2,64,1024]{2,1,0:T(8,128)(2,1)S(1)}, bf16[2,64,1024]{2,1,0:T(8,128)(2,1)S(1)}, u32[]{:S(2)}, u32[]{:S(2)}) collective-permute-start(bf16[2,64,1024]{2,1,0:T(8,128)(2,1)S(1)} %pad_maximum_fusion.refs_0_), channel_id=1, source_target_pairs={{0,8},{8,0},{16,24},{24,16},{1,9},{9,1},{17,25},{25,17},{2,10},{10... | collective-permute-start | bytes 786440 | tf_op jit(solution)/shard_map/ppermute | solution.py:247
  31.5 38.4 %all-to-all-start = ((bf16[32,8,2048]{2,1,0:T(8,128)(2,1)}), bf16[32,8,2048]{2,1,0:T(8,128)(2,1)S(1)}, u32[]{:S(2)}, u32[]{:S(2)}) async-start(bf16[32,8,2048]{2,1,0:T(8,128)(2,1)} %bitcast.3), calls=%async_computation | async-start | bytes 2097152 | tf_op jit(solution)/shard_map/all_to_all | solution.py:324
  38.1 17.9 %copy-start.1 = (bf16[1024,2048]{1,0:T(8,128)(2,1)S(1)}, bf16[1024,2048]{1,0:T(8,128)(2,1)}, u32[]{:S(2)}) copy-start(bf16[1024,2048]{1,0:T(8,128)(2,1)} %w_ref.3) | copy-start | bytes 12582916
  45.1 9.3 %collective-permute-start.2 = (bf16[1,64,1024]{2,1,0:T(8,128)(2,1)S(1)}, bf16[1,64,1024]{2,1,0:T(8,128)(2,1)S(1)}, u32[]{:S(2)}, u32[]{:S(2)}) collective-permute-start(bf16[1,64,1024]{2,1,0:T(8,128)(2,1)S(1)} %bitcast.20), channel_id=1, source_target_pairs={{0,16},{8,24},{16,0},{24,8},{1,17},{9,25},{17,1},{25,9},{2,18},{10... | collective-permute-start | bytes 393224 | tf_op jit(solution)/shard_map/ppermute | solution.py:247
  54.4 1.6 %collective-permute-start.3 = (bf16[2,64,1024]{2,1,0:T(8,128)(2,1)S(1)}, bf16[2,64,1024]{2,1,0:T(8,128)(2,1)S(1)}, u32[]{:S(2)}, u32[]{:S(2)}) collective-permute-start(bf16[2,64,1024]{2,1,0:T(8,128)(2,1)S(1)} %pad_maximum_fusion.1.refs_0_), channel_id=1, source_target_pairs={{0,8},{8,0},{16,24},{24,16},{1,9},{9,1},{17,25},{25,17},{2,10},{10... | collective-permute-start | bytes 786440 | tf_op jit(solution)/shard_map/ppermute | solution.py:247
  57.3 33.2 %copy-start.6 = (f32[16,8192]{1,0:T(8,128)S(1)}, f32[16,8192]{1,0:T(8,128)}, u32[]{:S(2)}) copy-start(f32[16,8192]{1,0:T(8,128)} %param.14) | copy-start | bytes 1572868
  57.4 9.2 %collective-permute-start.4 = (bf16[256,512]{1,0:T(8,128)(2,1)S(1)}, bf16[256,512]{1,0:T(8,128)(2,1)S(1)}, u32[]{:S(2)}, u32[]{:S(2)}) collective-permute-start(bf16[256,512]{1,0:T(8,128)(2,1)S(1)} %get-tuple-element.14), channel_id=1, source_target_pairs={{0,1},{1,0},{2,3},{3,2},{4,5},{5,4},{6,7},{7,6},{8,9},{9,8},{10,11... | collective-permute-start | bytes 786440 | tf_op jit(solution)/shard_map/ppermute | solution.py:247
  58.4 10.5 %collective-permute-start.5 = (bf16[256,512]{1,0:T(8,128)(2,1)S(1)}, bf16[256,512]{1,0:T(8,128)(2,1)S(1)}, u32[]{:S(2)}, u32[]{:S(2)}) collective-permute-start(bf16[256,512]{1,0:T(8,128)(2,1)S(1)} %get-tuple-element.15), channel_id=1, source_target_pairs={{0,2},{1,3},{2,0},{3,1},{4,6},{5,7},{6,4},{7,5},{8,10},{9,11},{10,... | collective-permute-start | bytes 786440 | tf_op jit(solution)/shard_map/ppermute | solution.py:247
  69.9 20.4 %all-to-all-start.1 = ((bf16[32,8,1024]{2,1,0:T(8,128)(2,1)}), bf16[32,8,1024]{2,1,0:T(8,128)(2,1)S(1)}, u32[]{:S(2)}, u32[]{:S(2)}) async-start(bf16[32,8,1024]{2,1,0:T(8,128)(2,1)} %fusion), calls=%async_computation.1 | async-start | bytes 1048576 | tf_op jit(solution)/shard_map/all_to_all | solution.py:324
where the time goes:
time: 90.4 us; the launch traced here: 91.5 us
  waiting for transfers between devices  33.8 us (37%)
  starting transfers between devices  26.5 us (29%)
  Pallas kernels  17.6 us (19%)
  blocking collectives  8.62 us (10%)
  other arithmetic  3.07 us (3%)
  local copies, waits for them, and re-layouts  1.63 us (2%)
    ppermute x6, waiting for transfers between devices, swapped(): lax.ppermute(value, axis, [(a, a ^ bit) for a in range(lax.axis_size(axis...  17.6 us
    all_to_all x2, waiting for transfers between devices, exchange(): return lax.all_to_all(sent, ('seq', 'head'), 0, 0)  16.2 us
    ppermute x6, starting transfers between devices, swapped(): lax.ppermute(value, axis, [(a, a ^ bit) for a in range(lax.axis_size(axis...  15.9 us
    pallas_call x2, Pallas kernels, attention(): pl.pallas_call(functools.partial(attention_kernel, token_at, skip, steps,...  14 us
    all_to_all x2, starting transfers between devices, exchange(): return lax.all_to_all(sent, ('seq', 'head'), 0, 0)  10.6 us
    all_gather x1, blocking collectives, context_blocks(): lax.all_gather(block, 'seq', axis=0, tiled=True)  8.62 us
    pallas_call x2, Pallas kernels, project(): pl.pallas_call(functools.partial(project_kernel, order, split), out_shape...  3.59 us
  transfers between devices with their start and end apart: 8, of which 7 were waited for; matrix products, arithmetic and copies ran while one was open for 1% of the time, Pallas kernels for 9%

commit v1 on v0

--- a/solution.py
+++ b/solution.py
@@ -21,7 +21,7 @@
 
 
 def attention_kernel(
-    token_at, skip, steps, most, tok, own_ref, base_ref, first_ref, q_hbm, ctx_hbm, *rest,
+    token_at, skip, steps, most, tok, ahead, first_ref, q_hbm, ctx_hbm, *rest,
     held,
 ):
     if held:
@@ -49,8 +49,9 @@
     for copy in copies:
         copy.wait()
     blocks = kx.shape[1] // BLOCK
-    own = own_ref[0]
-    base = base_ref[0]
+    place = lax.axis_index("seq")
+    own = place if ahead is None else ahead
+    base = place * tok
     origin = base - own * tok
     for b in range(blocks):
         rows = slice(b * BLOCK, (b + 1) * BLOCK)
@@ -167,7 +168,7 @@
         weight.wait()
 
 
-def attention(token_at, skip, steps, own, base, first_key, q, context, held=None):
+def attention(token_at, skip, steps, ahead, first_key, q, context, held=None):
     tok = first_key.shape[0]
     count = steps * GROUP * RUN
     rows = context.shape[0]
@@ -177,10 +178,12 @@
     unit = GROUPS * GROUP * ROWS
     more = [] if held is None else [held]
     out = pl.pallas_call(
-        functools.partial(attention_kernel, token_at, skip, steps, most, tok, held=held is not None),
+        functools.partial(
+            attention_kernel, token_at, skip, steps, most, tok, ahead, held=held is not None
+        ),
         out_shape=[jax.ShapeDtypeStruct((count, TILE * DH), bf16)]
         + [jax.ShapeDtypeStruct(value.shape, value.dtype) for value in more],
-        in_specs=[pl.BlockSpec(memory_space=pltpu.SMEM)] * 3
+        in_specs=[pl.BlockSpec(memory_space=pltpu.SMEM)]
         + [pl.BlockSpec(memory_space=pl.ANY)] * (2 + len(more)),
         out_specs=[pl.BlockSpec(memory_space=pltpu.VMEM)]
         + [pl.BlockSpec(memory_space=pl.ANY) for value in more],
@@ -204,16 +207,15 @@
         ),
         compiler_params=pltpu.CompilerParams(vmem_limit_bytes=30 * 2**20),
         name="attention",
-    )(own, base, first_key, q, context, *more)
+    )(first_key, q, context, *more)
     return out if more else out[0]
 
 
 def project_kernel(order, split, w_ref, *refs):
     me, head = lax.axis_index("seq"), lax.axis_index("head")
     bits = [head % 2, head // 2 % 2]
-    kept_ref, came_ref, *outs, rows_ref = refs
-    count = kept_ref.shape[1]
-    pieces = [ref.at[i] for ref in (kept_ref, came_ref) for i in range(ref.shape[0])]
+    pieces, outs, rows_ref = refs[: len(order)], refs[len(order) : -1], refs[-1]
+    count = pieces[0].shape[0]
     for other, piece in zip(order, pieces, strict=True):
         at = pl.multiple_of((me ^ other) * count, count)
         rows_ref[pl.ds(at, count)] = piece[...]
@@ -249,13 +251,11 @@
 
 def project(features, out_weight, split=False):
     size = lax.axis_size("seq")
-    kept, order, bit = features[None], [0], size // 2
+    pieces, bit = {0: features}, size // 2
     while bit:
-        came = swapped(kept, "seq", bit)
-        order = order + [other ^ bit for other in order]
+        for other, piece in list(pieces.items()):
+            pieces[other ^ bit] = swapped(piece, "seq", bit)
         bit //= 2
-        if bit:
-            kept = jnp.concatenate([kept, came], axis=0)
     rows = size * features.shape[0]
     depth, columns = out_weight.shape
     shapes = jax.ShapeDtypeStruct((rows, columns), jnp.bfloat16)
@@ -264,9 +264,9 @@
         shapes = [jax.ShapeDtypeStruct((rows, columns // 2), jnp.float32)]
         shapes += [jax.ShapeDtypeStruct((rows, columns // 4), jnp.bfloat16)] * 2
     return pl.pallas_call(
-        functools.partial(project_kernel, order, split),
+        functools.partial(project_kernel, list(pieces), split),
         out_shape=shapes,
-        in_specs=[pl.BlockSpec(memory_space=pltpu.VMEM)] * 3,
+        in_specs=[pl.BlockSpec(memory_space=pltpu.VMEM)] * (1 + len(pieces)),
         out_specs=[memory] * 3 if split else memory,
         scratch_shapes=[pltpu.VMEM((rows, depth), jnp.bfloat16)],
         cost_estimate=pl.CostEstimate(
@@ -274,18 +274,18 @@
         ),
         compiler_params=pltpu.CompilerParams(vmem_limit_bytes=20 * 2**20),
         name="project",
-    )(out_weight, kept, came)
+    )(out_weight, *pieces.values())
 
 
 def context_blocks(block, reach):
     count = lax.axis_size("seq")
     if count <= reach + 1:
-        return lax.all_gather(block, "seq", axis=0, tiled=True), lax.axis_index("seq")
+        return lax.all_gather(block, "seq", axis=0, tiled=True), None
     pieces = [
         lax.ppermute(block, "seq", [(a, a + steps) for a in range(count - steps)])
         for steps in range(reach, 0, -1)
     ]
-    return jnp.concatenate(pieces + [block], axis=0), jnp.int32(reach)
+    return jnp.concatenate(pieces + [block], axis=0), reach
 
 
 def local(queries, key_rows, value_rows, pair_keys, pair_values, first_key, residual, out_weight):
@@ -293,20 +293,18 @@
     width = queries.shape[1]
     seq_size, head_size = lax.axis_size("seq"), lax.axis_size("head")
     block = jnp.concatenate([key_rows, value_rows, pair_keys, pair_values], axis=1)
-    context, own = context_blocks(block, (W1 + tok - 1) // tok)
-    base = lax.axis_index("seq") * tok
-    own, base = (jnp.asarray(value, jnp.int32).reshape(1) for value in (own, base))
+    context, ahead = context_blocks(block, (W1 + tok - 1) // tok)
     tile = TILE * DH
 
     step = GROUP * RUN
 
-    def attend(start, skip, steps, base):
+    def attend(start, skip, steps, context):
         parts = []
         for at in range(0, width, tile):
             q = queries[:, at : at + tile]
             if q.shape[1] < tile:
                 q = jnp.pad(q, ((0, 0), (0, tile - q.shape[1])))
-            parts.append(attention(start, skip, steps, own, base, first_key, q, context))
+            parts.append(attention(start, skip, steps, ahead, first_key, q, context))
         return (parts[0] if len(parts) == 1 else jnp.concatenate(parts, axis=1))[:, :width]
 
     columns = out_weight.shape[1]
@@ -336,14 +334,14 @@
         return jnp.moveaxis(both, 3, 0).reshape(-1, seq_size * columns)
 
     if rows != 2 * step or head_size % 4:
-        sent = product(attend(0, step, tok // step, base), rows)
+        sent = product(attend(0, step, tok // step, context), rows)
         return residual + total(exchange(sent))
     steps = tok // rows
-    first = attend(0, rows, steps, base)
+    first = attend(0, rows, steps, context)
     sent = product(first, step)
-    base, sent = lax.optimization_barrier((base, sent))
+    context, sent = lax.optimization_barrier((context, sent))
     got_first = exchange(sent)
-    second = attend(step, rows, steps, base)
+    second = attend(step, rows, steps, context)
     kept, *leaving = product(second, step, True)
     came = [swapped(value, "head", bit) for value, bit in zip(leaving, (1, 2), strict=True)]
     sent, got_first = lax.optimization_barrier((add_pairs(kept, came), got_first))

time: 90.4 us -> 91.7 us (1.014)
  starting transfers between devices: 26.5 us -> 28.1 us
    ppermute x6 -> x8, starting transfers between devices: 15.9 us -> 17.5 us  [swapped(): lax.ppermute(value, axis, [(a, a ^ bit) for a in range(lax.axis_size(axis...]
    ppermute x6 -> x8, waiting for transfers between devices: 17.6 us -> 17.3 us  [swapped(): lax.ppermute(value, axis, [(a, a ^ bit) for a in range(lax.axis_size(axis...]
  transfers between devices with their start and end apart: 8 -> 10, of which waited for: 7 -> 7; matrix products, arithmetic and copies ran while one was open for 1% -> 1% of each run, Pallas kernels for 9% -> 9%
where the time goes in v1:
time: 91.7 us; the launch traced here: 92.5 us
  waiting for transfers between devices  33.5 us (37%)
  starting transfers between devices  28.1 us (31%)
  Pallas kernels  17.5 us (19%)
  blocking collectives  8.62 us (9%)
  other arithmetic  3.02 us (3%)
  local copies, waits for them, and re-layouts  1.63 us (2%)
    ppermute x8, starting transfers between devices, swapped(): lax.ppermute(value, axis, [(a, a ^ bit) for a in range(lax.axis_size(axis...  17.5 us
    ppermute x8, waiting for transfers between devices, swapped(): lax.ppermute(value, axis, [(a, a ^ bit) for a in range(lax.axis_size(axis...  17.3 us
    all_to_all x2, waiting for transfers between devices, exchange(): return lax.all_to_all(sent, ('seq', 'head'), 0, 0)  16.2 us
    pallas_call x2, Pallas kernels, attention(): pl.pallas_call(functools.partial(attention_kernel, token_at, skip, steps,...  14 us
    all_to_all x2, starting transfers between devices, exchange(): return lax.all_to_all(sent, ('seq', 'head'), 0, 0)  10.6 us
    all_gather x1, blocking collectives, context_blocks(): return (lax.all_gather(block, 'seq', axis=0, tiled=True), None)  8.62 us
    pallas_call x2, Pallas kernels, project(): pl.pallas_call(functools.partial(project_kernel, list(pieces), split), ou...  3.56 us
  transfers between devices with their start and end apart: 10, of which 7 were waited for; matrix products, arithmetic and copies ran while one was open for 1% of the time, Pallas kernels for 9%

profile of v1, /device:TPU:0, one launch (start us, length us, event | category | flops | bytes accessed | tf_op | source)
XLA Modules:
  0.0 92.5 jit_solution(6537685042037670961)
XLA Ops:
  0.0 0.8 pad_maximum_fusion.1
  0.8 8.6 %all_gather.3.ctx_hbm = bf16[512,512]{1,0:T(8,128)(2,1)S(1)} all-gather(bf16[128,512]{1,0:T(8,128)(2,1)S(1)} %pad_maximum_fusion.1), channel_id=1, replica_groups=mesh['seq'=4,'head'=8] {'seq'}, dimensions={0}, use_global_device_ids=true | all-gather | bytes 655360 | tf_op jit(solution)/shard_map/all_gather | solution.py:283
  9.4 0.0 copy-start.2
  9.4 0.9 %copy-done.2 = bf16[128,1024]{1,0:T(8,128)(2,1)S(1)} copy-done((bf16[128,1024]{1,0:T(8,128)(2,1)S(1)}, bf16[128,1024]{1,0:T(8,128)(2,1)}, u32[]{:S(2)}) %copy-start.2) | copy-done | bytes 262168
  10.4 0.0 copy-start.4
  10.4 0.7 copy-done.4
  11.1 0.0 copy-start
  11.1 7.0 %attention.2.refs_0_ = bf16[64,1024]{1,0:T(8,128)(2,1)S(1)} custom-call(s32[128]{0:T(128)S(1)} %copy-done.4, bf16[128,1024]{1,0:T(8,128)(2,1)S(1)} %copy-done.2, bf16[512,512]{1,0:T(8,128)(2,1)S(1)} %all_gather.3.ctx_hbm), custom_call_target="tpu_custom_call" | custom-call | flops 8589934592 | bytes 1048576 | tf_op jit(solution)/shard_map/attention/pallas_call | solution.py:180
  18.0 0.0 copy-start.3
  18.1 0.0 copy-start.5
  18.1 6.6 %collective-permute-start = (bf16[64,1024]{1,0:T(8,128)(2,1)S(1)}, bf16[64,1024]{1,0:T(8,128)(2,1)S(1)}, u32[]{:S(2)}, u32[]{:S(2)}) collective-permute-start(bf16[64,1024]{1,0:T(8,128)(2,1)S(1)} %attention.2.refs_0_), channel_id=1, source_target_pairs={{0,16},{8,24},{16,0},{24,8},{1,17},{9,25},{17,1},{25,9},{2,18},{10... | collective-permute-start | bytes 393224 | tf_op jit(solution)/shard_map/ppermute | solution.py:249
  24.6 0.0 collective-permute-start.1
  24.6 3.5 %collective-permute-done.refs_1_ = bf16[64,1024]{1,0:T(8,128)(2,1)S(1)} collective-permute-done((bf16[64,1024]{1,0:T(8,128)(2,1)S(1)}, bf16[64,1024]{1,0:T(8,128)(2,1)S(1)}, u32[]{:S(2)}, u32[]{:S(2)}) %collective-permute-start) | collective-permute-done | bytes 131104 | tf_op jit(solution)/shard_map/ppermute | solution.py:249
  28.1 0.0 collective-permute-start.2
  28.2 0.0 collective-permute-done.1.refs_2_
  28.2 1.3 %collective-permute-done.2.refs_3_ = bf16[64,1024]{1,0:T(8,128)(2,1)S(1)} collective-permute-done((bf16[64,1024]{1,0:T(8,128)(2,1)S(1)}, bf16[64,1024]{1,0:T(8,128)(2,1)S(1)}, u32[]{:S(2)}, u32[]{:S(2)}) %collective-permute-start.2) | collective-permute-done | bytes 131104 | tf_op jit(solution)/shard_map/ppermute | solution.py:249
  29.5 0.0 copy-done
  29.5 2.3 %project.2 = bf16[256,2048]{1,0:T(8,128)(2,1)} custom-call(bf16[1024,2048]{1,0:T(8,128)(2,1)S(1)} %copy-done, bf16[64,1024]{1,0:T(8,128)(2,1)S(1)} %attention.2.refs_0_, bf16[64,1024]{1,0:T(8,128)(2,1)S(1)} %collective-permute-done.refs_1_, bf16[64,1024]{1,0:T(8,128)(2,1)S(1)} %collective-permute-done.1.refs_2_, ...), custom_call_target="tpu_custom_call" | custom-call | flops 1073741824 | bytes 4194304 | tf_op jit(solution)/shard_map/project/pallas_call | solution.py:266
  31.8 6.3 %all-to-all-start = ((bf16[32,8,2048]{2,1,0:T(8,128)(2,1)}), bf16[32,8,2048]{2,1,0:T(8,128)(2,1)S(1)}, u32[]{:S(2)}, u32[]{:S(2)}) async-start(bf16[32,8,2048]{2,1,0:T(8,128)(2,1)} %bitcast), calls=%async_computation | async-start | bytes 2097152 | tf_op jit(solution)/shard_map/all_to_all | solution.py:322
  38.0 0.0 copy-done.3
  38.0 0.0 copy-done.5
  38.1 0.0 copy-start.1
  38.1 7.0 %attention.3.refs_0_ = bf16[64,1024]{1,0:T(8,128)(2,1)S(1)} custom-call(s32[128]{0:T(128)S(1)} %copy-done.5, bf16[128,1024]{1,0:T(8,128)(2,1)S(1)} %copy-done.3, bf16[512,512]{1,0:T(8,128)(2,1)S(1)} %all_gather.3.ctx_hbm), custom_call_target="tpu_custom_call" | custom-call | flops 8589934592 | bytes 1048576 | tf_op jit(solution)/shard_map/attention/pallas_call | solution.py:180
  45.1 7.1 %collective-permute-start.3 = (bf16[64,1024]{1,0:T(8,128)(2,1)S(1)}, bf16[64,1024]{1,0:T(8,128)(2,1)S(1)}, u32[]{:S(2)}, u32[]{:S(2)}) collective-permute-start(bf16[64,1024]{1,0:T(8,128)(2,1)S(1)} %attention.3.refs_0_), channel_id=1, source_target_pairs={{0,16},{8,24},{16,0},{24,8},{1,17},{9,25},{17,1},{25,9},{2,18},{10... | collective-permute-start | bytes 393224 | tf_op jit(solution)/shard_map/ppermute | solution.py:249
  52.1 0.0 collective-permute-start.4
  52.1 4.3 %collective-permute-done.3.refs_1_ = bf16[64,1024]{1,0:T(8,128)(2,1)S(1)} collective-permute-done((bf16[64,1024]{1,0:T(8,128)(2,1)S(1)}, bf16[64,1024]{1,0:T(8,128)(2,1)S(1)}, u32[]{:S(2)}, u32[]{:S(2)}) %collective-permute-start.3) | collective-permute-done | bytes 131104 | tf_op jit(solution)/shard_map/ppermute | solution.py:249
  56.5 0.0 collective-permute-start.5
  56.5 0.0 collective-permute-done.4.refs_2_
  56.5 1.3 %collective-permute-done.5.refs_3_ = bf16[64,1024]{1,0:T(8,128)(2,1)S(1)} collective-permute-done((bf16[64,1024]{1,0:T(8,128)(2,1)S(1)}, bf16[64,1024]{1,0:T(8,128)(2,1)S(1)}, u32[]{:S(2)}, u32[]{:S(2)}) %collective-permute-start.5) | collective-permute-done | bytes 131104 | tf_op jit(solution)/shard_map/ppermute | solution.py:249
  57.8 0.0 copy-done.1
  57.8 1.3 %project.3 = (f32[256,1024]{1,0:T(8,128)S(1)}, bf16[256,512]{1,0:T(8,128)(2,1)S(1)}, bf16[256,512]{1,0:T(8,128)(2,1)S(1)}) custom-call(bf16[1024,2048]{1,0:T(8,128)(2,1)S(1)} %copy-done.1, bf16[64,1024]{1,0:T(8,128)(2,1)S(1)} %attention.3.refs_0_, bf16[64,1024]{1,0:T(8,128)(2,1)S(1)} %collective-permute-done.3.refs_1_, ...), custom_call_target="tpu_custom_call" | custom-call | flops 1073741824 | bytes 4194304 | tf_op jit(solution)/shard_map/project/pallas_call | solution.py:266
  59.1 0.0 copy-start.6
  59.1 1.7 %collective-permute-start.6 = (bf16[256,512]{1,0:T(8,128)(2,1)S(1)}, bf16[256,512]{1,0:T(8,128)(2,1)S(1)}, u32[]{:S(2)}, u32[]{:S(2)}) collective-permute-start(bf16[256,512]{1,0:T(8,128)(2,1)S(1)} %get-tuple-element.14), channel_id=1, source_target_pairs={{0,1},{1,0},{2,3},{3,2},{4,5},{5,4},{6,7},{7,6},{8,9},{9,8},{10,11... | collective-permute-start | bytes 786440 | tf_op jit(solution)/shard_map/ppermute | solution.py:249
  60.9 2.1 %collective-permute-start.7 = (bf16[256,512]{1,0:T(8,128)(2,1)S(1)}, bf16[256,512]{1,0:T(8,128)(2,1)S(1)}, u32[]{:S(2)}, u32[]{:S(2)}) collective-permute-start(bf16[256,512]{1,0:T(8,128)(2,1)S(1)} %get-tuple-element.15), channel_id=1, source_target_pairs={{0,2},{1,3},{2,0},{3,1},{4,6},{5,7},{6,4},{7,5},{8,10},{9,11},{10,... | collective-permute-start | bytes 786440 | tf_op jit(solution)/shard_map/ppermute | solution.py:249
  63.0 5.4 %collective-permute-done.6 = bf16[256,512]{1,0:T(8,128)(2,1)S(1)} collective-permute-done((bf16[256,512]{1,0:T(8,128)(2,1)S(1)}, bf16[256,512]{1,0:T(8,128)(2,1)S(1)}, u32[]{:S(2)}, u32[]{:S(2)}) %collective-permute-start.6) | collective-permute-done | bytes 262176 | tf_op jit(solution)/shard_map/ppermute | solution.py:249
  68.4 1.3 %collective-permute-done.7 = bf16[256,512]{1,0:T(8,128)(2,1)S(1)} collective-permute-done((bf16[256,512]{1,0:T(8,128)(2,1)S(1)}, bf16[256,512]{1,0:T(8,128)(2,1)S(1)}, u32[]{:S(2)}, u32[]{:S(2)}) %collective-permute-start.7) | collective-permute-done | bytes 262176 | tf_op jit(solution)/shard_map/ppermute | solution.py:249
  69.7 0.9 %fusion = bf16[32,8,1024]{2,1,0:T(8,128)(2,1)} fusion(f32[256,1024]{1,0:T(8,128)S(1)} %get-tuple-element.13, bf16[256,512]{1,0:T(8,128)(2,1)S(1)} %collective-permute-done.7, bf16[256,512]{1,0:T(8,128)(2,1)S(1)} %collective-permute-done.6), kind=kLoop, calls=%fused_computation.2 | loop fusion | flops 1572864 | bytes 2097152 | tf_op jit(solution)/shard_map/reshape | solution.py:319
  70.6 0.0 all-to-all-done
  70.6 4.3 %all-to-all-start.1 = ((bf16[32,8,1024]{2,1,0:T(8,128)(2,1)}), bf16[32,8,1024]{2,1,0:T(8,128)(2,1)S(1)}, u32[]{:S(2)}, u32[]{:S(2)}) async-start(bf16[32,8,1024]{2,1,0:T(8,128)(2,1)} %fusion), calls=%async_computation.1 | async-start | bytes 1048576 | tf_op jit(solution)/shard_map/all_to_all | solution.py:322
  75.0 0.2 convert_reduce_fusion
  75.1 16.2 %all-to-all-done.1 = bf16[32,8,1024]{2,1,0:T(8,128)(2,1)S(1)} async-done(((bf16[32,8,1024]{2,1,0:T(8,128)(2,1)}), bf16[32,8,1024]{2,1,0:T(8,128)(2,1)S(1)}, u32[]{:S(2)}, u32[]{:S(2)}) %all-to-all-start.1) | async-done | bytes 524320 | tf_op jit(solution)/shard_map/all_to_all | solution.py:322
  91.3 0.1 convert.2
  91.4 0.1 slice_reduce_fusion.1
  91.6 0.0 copy-done.6
  91.6 0.9 maximum_add_fusion
  (1 shorter events, 0.0 us)
Async XLA Ops:
  9.4 0.9 %copy-start.2 = (bf16[128,1024]{1,0:T(8,128)(2,1)S(1)}, bf16[128,1024]{1,0:T(8,128)(2,1)}, u32[]{:S(2)}) copy-start(bf16[128,1024]{1,0:T(8,128)(2,1)} %q_hbm.3) | copy-start | bytes 786436
  10.4 0.7 copy-start.4
  11.1 18.4 %copy-start = (bf16[1024,2048]{1,0:T(8,128)(2,1)S(1)}, bf16[1024,2048]{1,0:T(8,128)(2,1)}, u32[]{:S(2)}) copy-start(bf16[1024,2048]{1,0:T(8,128)(2,1)} %w_ref.3) | copy-start | bytes 12582916
  18.0 20.0 %copy-start.3 = (bf16[128,1024]{1,0:T(8,128)(2,1)S(1)}, bf16[128,1024]{1,0:T(8,128)(2,1)}, u32[]{:S(2)}) copy-start(bf16[128,1024]{1,0:T(8,128)(2,1)} %q_hbm.3) | copy-start | bytes 786436
  18.1 20.0 %copy-start.5 = (s32[128]{0:T(128)S(1)}, s32[128]{0:T(128)}, u32[]{:S(2)}) copy-start(s32[128]{0:T(128)} %first_ref.3) | copy-start | bytes 1540
  18.1 10.1 %collective-permute-start = (bf16[64,1024]{1,0:T(8,128)(2,1)S(1)}, bf16[64,1024]{1,0:T(8,128)(2,1)S(1)}, u32[]{:S(2)}, u32[]{:S(2)}) collective-permute-start(bf16[64,1024]{1,0:T(8,128)(2,1)S(1)} %attention.2.refs_0_), channel_id=1, source_target_pairs={{0,16},{8,24},{16,0},{24,8},{1,17},{9,25},{17,1},{25,9},{2,18},{10... | collective-permute-start | bytes 393224 | tf_op jit(solution)/shard_map/ppermute | solution.py:249
  24.6 3.5 %collective-permute-start.1 = (bf16[64,1024]{1,0:T(8,128)(2,1)S(1)}, bf16[64,1024]{1,0:T(8,128)(2,1)S(1)}, u32[]{:S(2)}, u32[]{:S(2)}) collective-permute-start(bf16[64,1024]{1,0:T(8,128)(2,1)S(1)} %attention.2.refs_0_), channel_id=1, source_target_pairs={{0,8},{8,0},{16,24},{24,16},{1,9},{9,1},{17,25},{25,17},{2,10},{10... | collective-permute-start | bytes 393224 | tf_op jit(solution)/shard_map/ppermute | solution.py:249
  28.1 1.3 %collective-permute-start.2 = (bf16[64,1024]{1,0:T(8,128)(2,1)S(1)}, bf16[64,1024]{1,0:T(8,128)(2,1)S(1)}, u32[]{:S(2)}, u32[]{:S(2)}) collective-permute-start(bf16[64,1024]{1,0:T(8,128)(2,1)S(1)} %collective-permute-done.refs_1_), channel_id=1, source_target_pairs={{0,8},{8,0},{16,24},{24,16},{1,9},{9,1},{17,25},{25,17},{2,10},{10... | collective-permute-start | bytes 393224 | tf_op jit(solution)/shard_map/ppermute | solution.py:249
  31.8 38.9 %all-to-all-start = ((bf16[32,8,2048]{2,1,0:T(8,128)(2,1)}), bf16[32,8,2048]{2,1,0:T(8,128)(2,1)S(1)}, u32[]{:S(2)}, u32[]{:S(2)}) async-start(bf16[32,8,2048]{2,1,0:T(8,128)(2,1)} %bitcast), calls=%async_computation | async-start | bytes 2097152 | tf_op jit(solution)/shard_map/all_to_all | solution.py:322
  38.1 19.8 %copy-start.1 = (bf16[1024,2048]{1,0:T(8,128)(2,1)S(1)}, bf16[1024,2048]{1,0:T(8,128)(2,1)}, u32[]{:S(2)}) copy-start(bf16[1024,2048]{1,0:T(8,128)(2,1)} %w_ref.3) | copy-start | bytes 12582916
  45.1 11.4 %collective-permute-start.3 = (bf16[64,1024]{1,0:T(8,128)(2,1)S(1)}, bf16[64,1024]{1,0:T(8,128)(2,1)S(1)}, u32[]{:S(2)}, u32[]{:S(2)}) collective-permute-start(bf16[64,1024]{1,0:T(8,128)(2,1)S(1)} %attention.3.refs_0_), channel_id=1, source_target_pairs={{0,16},{8,24},{16,0},{24,8},{1,17},{9,25},{17,1},{25,9},{2,18},{10... | collective-permute-start | bytes 393224 | tf_op jit(solution)/shard_map/ppermute | solution.py:249
  52.1 4.4 %collective-permute-start.4 = (bf16[64,1024]{1,0:T(8,128)(2,1)S(1)}, bf16[64,1024]{1,0:T(8,128)(2,1)S(1)}, u32[]{:S(2)}, u32[]{:S(2)}) collective-permute-start(bf16[64,1024]{1,0:T(8,128)(2,1)S(1)} %attention.3.refs_0_), channel_id=1, source_target_pairs={{0,8},{8,0},{16,24},{24,16},{1,9},{9,1},{17,25},{25,17},{2,10},{10... | collective-permute-start | bytes 393224 | tf_op jit(solution)/shard_map/ppermute | solution.py:249
  56.5 1.3 %collective-permute-start.5 = (bf16[64,1024]{1,0:T(8,128)(2,1)S(1)}, bf16[64,1024]{1,0:T(8,128)(2,1)S(1)}, u32[]{:S(2)}, u32[]{:S(2)}) collective-permute-start(bf16[64,1024]{1,0:T(8,128)(2,1)S(1)} %collective-permute-done.3.refs_1_), channel_id=1, source_target_pairs={{0,8},{8,0},{16,24},{24,16},{1,9},{9,1},{17,25},{25,17},{2,10},{10... | collective-permute-start | bytes 393224 | tf_op jit(solution)/shard_map/ppermute | solution.py:249
  59.1 32.5 %copy-start.6 = (f32[16,8192]{1,0:T(8,128)S(1)}, f32[16,8192]{1,0:T(8,128)}, u32[]{:S(2)}) copy-start(f32[16,8192]{1,0:T(8,128)} %param.14) | copy-start | bytes 1572868
  59.1 9.3 %collective-permute-start.6 = (bf16[256,512]{1,0:T(8,128)(2,1)S(1)}, bf16[256,512]{1,0:T(8,128)(2,1)S(1)}, u32[]{:S(2)}, u32[]{:S(2)}) collective-permute-start(bf16[256,512]{1,0:T(8,128)(2,1)S(1)} %get-tuple-element.14), channel_id=1, source_target_pairs={{0,1},{1,0},{2,3},{3,2},{4,5},{5,4},{6,7},{7,6},{8,9},{9,8},{10,11... | collective-permute-start | bytes 786440 | tf_op jit(solution)/shard_map/ppermute | solution.py:249
  60.9 8.8 %collective-permute-start.7 = (bf16[256,512]{1,0:T(8,128)(2,1)S(1)}, bf16[256,512]{1,0:T(8,128)(2,1)S(1)}, u32[]{:S(2)}, u32[]{:S(2)}) collective-permute-start(bf16[256,512]{1,0:T(8,128)(2,1)S(1)} %get-tuple-element.15), channel_id=1, source_target_pairs={{0,2},{1,3},{2,0},{3,1},{4,6},{5,7},{6,4},{7,5},{8,10},{9,11},{10,... | collective-permute-start | bytes 786440 | tf_op jit(solution)/shard_map/ppermute | solution.py:249
  70.6 20.7 %all-to-all-start.1 = ((bf16[32,8,1024]{2,1,0:T(8,128)(2,1)}), bf16[32,8,1024]{2,1,0:T(8,128)(2,1)S(1)}, u32[]{:S(2)}, u32[]{:S(2)}) async-start(bf16[32,8,1024]{2,1,0:T(8,128)(2,1)} %fusion), calls=%async_computation.1 | async-start | bytes 1048576 | tf_op jit(solution)/shard_map/all_to_all | solution.py:322
